TPU v7x, 32 devices: a whole 2x2x4 slice. The times are simulated.
32 devices in a mesh: group: 2 (over y), chan: 4 (over z), frame: 2 (over x), sub: 2 (over core).
Axes of the slice: x: 2, y: 2, z: 4, core: 2. Of those that a mesh axis runs over, the one named last changes fastest.
Arguments:
- rf: bfloat16 [32768, 512], P(('group', 'chan', 'sub'), 'frame'), parts along dimension 0, may hold values from -10 to 10
- weights: bfloat16 [8, 2, 2, 128, 128], P(('chan', 'sub')), may hold values from -0.125 to 0.125
- sample_block: int32 [8, 2, 2], P(('chan', 'sub')), may hold values from 0 to 15
- live: int32 [8, 2, 2], P(('chan', 'sub')), may hold values 0 or 1
- rank: int32 [2], P('group'), parts along dimension 0, may hold values from 16 to 32
Outputs:
- power: float32 [16, 2, 16], P(('group', 'chan', 'sub'), 'frame'), parts along dimension 0
There are 2 independent parts, one for each index of `group`. A program takes and returns all parts, laid end to end along the dimension named above; an argument that names none is the same for every part. Nothing has to cross between parts.
Inputs may be any that keep to these rules, and one draw needn't show every extreme that they name: `sample_block`: index of a delay window within the channel's trace. `rank`: number of leading basis columns removed as clutter.
All inputs are finite; a program needn't handle non-finite values. No bound on the sum of `live` on one device may be relied on, other than what follows from the above.
Results may differ from a plain program's by a relative error of at most 0.0003.
Values sent between devices are 32-bit elements; how exact they have to be, the bound alone decides.
A program may use at most 64 MiB of HBM per device.

v0:
```python
import math

import jax
import jax.numpy as jnp
from jax import lax
from jax.sharding import PartitionSpec as P

F = 512
RMAX = 32


def start_basis():
    frames = jnp.arange(F, dtype=jnp.float32)[:, None] + 0.5
    orders = jnp.arange(RMAX, dtype=jnp.float32)[None, :]
    return jnp.cos(math.pi * frames * orders / F) * math.sqrt(2.0 / F)


def clutter_basis(subspace, rank):
    keep = (jnp.arange(RMAX) < rank[0]).astype(jnp.float32)
    masked = subspace * keep[None, :]
    matrix = jnp.dot(masked.T, masked, precision=lax.Precision.HIGHEST) + jnp.diag(1.0 - keep)
    lower = jnp.linalg.cholesky(matrix)
    return lax.linalg.triangular_solve(lower, masked, left_side=False, lower=True, transpose_a=True)


def shards(rf, weights, sample_block, live, rank):
    weight_set = weights[0]
    index_set = sample_block[0]
    live_set = live[0]
    block_rows = weight_set.shape[2]
    vox_block = weight_set.shape[3]
    num_blocks = weight_set.shape[0]
    frame_cols = rf.shape[1]
    blocks = rf.reshape(rf.shape[0] // block_rows, block_rows, frame_cols)
    total_vox = num_blocks * vox_block
    n_cs = lax.axis_size(("chan", "sub"))
    count_blocks = max(total_vox // n_cs * lax.axis_size(("chan", "sub")) // vox_block, 1)
    gathered = jnp.take(blocks, index_set, axis=0)
    masked = weight_set * live_set[:, :, None, None].astype(jnp.bfloat16)
    out = jnp.einsum("bpsc,bpsf->bcf", masked, gathered, preferred_element_type=jnp.float32)
    out = out.reshape(count_blocks * vox_block, frame_cols)
    owned = lax.psum_scatter(out, ("chan", "sub"), scatter_dimension=0, tiled=True)
    signal = lax.all_to_all(owned, "frame", split_axis=0, concat_axis=1, tiled=True)
    start = start_basis()
    local_gram = jnp.dot(signal.T, signal, precision=lax.Precision.HIGHEST)
    gram = lax.psum(local_gram, ("chan", "frame", "sub"))
    subspace = jnp.dot(gram, start, precision=lax.Precision.HIGHEST)
    basis = clutter_basis(subspace, rank)
    coeffs = jnp.dot(signal, basis, precision=lax.Precision.HIGHEST)
    clean = signal - jnp.dot(coeffs, basis.T, precision=lax.Precision.HIGHEST)
    power = jnp.mean(clean * clean, axis=1)
    return power.reshape(1, 1, power.shape[0])


def solution(mesh):
    return jax.shard_map(
        shards,
        mesh=mesh,
        in_specs=(
            P(("group", "chan", "sub"), "frame"),
            P(("chan", "sub"), None, None, None, None),
            P(("chan", "sub"), None, None),
            P(("chan", "sub"), None, None),
            P("group"),
        ),
        out_specs=P(("group", "chan", "sub"), "frame", None),
        check_vma=False,
    )
```

profile of v0, /device:TPU:0, one launch (start us, length us, event | category | flops | bytes accessed | tf_op | source)
XLA Modules:
  0.0 161.7 jit_solution(2042319083445673912)
XLA Ops:
  6.5 0.8 compare_select_fusion
  7.3 0.1 reshape.92
  7.4 0.7 copy-done.3
  8.1 0.6 gather_fusion
  8.7 0.3 copy-done.1
  9.0 1.0 fusion.7
  10.0 0.0 reduce-scatter.2.cloned.1.call-update
  10.0 0.0 all-reduce.2.cloned.1.call-start
  10.1 33.1 %reduce-scatter.2.cloned.1.call-done = f32[32,256]{1,0:T(8,128)} async-done(((f32[256,256]{1,0:T(8,128)}), f32[32,256]{1,0:T(8,128)}) %reduce-scatter.2.cloned.1.call-update) | async-done | bytes 32784 | tf_op jit(solution)/shard_map/reduce_scatter | solution.py:42
  43.2 7.2 %all_to_all.19 = f32[2,16,256]{2,1,0:T(8,128)S(1)} all-to-all(f32[2,16,256]{2,1,0:T(8,128)} %bitcast.54), channel_id=1, replica_groups=mesh['group'=2,'chan'=4,'frame'=2,'sub'=2] {'frame'}, dimensions={0} | all-to-all | bytes 65536 | tf_op jit(solution)/shard_map/all_to_all | solution.py:43
  50.4 2.1 %fusion.23 = f32[512,512]{1,0:T(8,128)} fusion(f32[16,512]{1,0:T(8,128)S(1)} %bitcast.50), kind=kOutput, calls=%fused_computation.43 | convolution fusion | flops 50331648 | bytes 1081344 | tf_op jit(solution)/shard_map/dot_general | solution.py:45
  53.2 90.2 %all-reduce.2.cloned.1.call-done = f32[512,512]{1,0:T(8,128)} async-done(((f32[512,512]{1,0:T(8,128)}), f32[512,512]{1,0:T(8,128)}) %all-reduce.2.cloned.1.call-update) | async-done | bytes 1048592 | tf_op jit(solution)/shard_map/psum | solution.py:46
  143.3 3.2 %convolution_multiply_fusion = f32[512,32]{0,1:T(8,128)S(1)} fusion(f32[512,512]{1,0:T(8,128)} %all-reduce.2.cloned.1.call-done, f32[512]{0:T(512)S(1)} %add_multiply_fusion, f32[32]{0:T(128)S(1)} %compare_convert_fusion), kind=kOutput, calls=%fused_computation.1 | convolution fusion | flops 100728832 | bytes 1116288 | tf_op jit(solution)/shard_map/dot_general | solution.py:47
  146.6 0.2 fusion.24
  146.8 0.1 copy.11
  146.8 0.1 fusion.19
  146.9 2.9 %cholesky.16 = f32[32,32]{1,0:T(8,128)S(1)} custom-call(f32[32,32]{1,0:T(8,128)S(1)} %fusion.19), custom_call_target="Cholesky" | custom-call | tf_op jit(solution)/shard_map/jit(cholesky)/cholesky | solution.py:22
  149.9 0.6 compare_reduce_fusion
  150.5 0.7 fusion.15
  151.2 2.4 %custom-call.6 = f32[1,32,32]{1,2,0:T(8,128)S(1)} custom-call(f32[1,32,32]{2,1,0:T(8,128)S(1)} %fusion.15), custom_call_target="InvertDiagBlocksLowerTriangular" | custom-call | tf_op jit(solution)/shard_map/triangular_solve | solution.py:23
  153.6 0.3 fusion.16
  153.9 0.2 fusion.25
  154.0 0.3 fusion.1
  154.3 0.5 multiply_bitcast_fusion
  (16 shorter events, 0.1 us)
Async XLA Ops:
  6.5 1.6 copy-start
  6.5 0.8 copy-start.2
  6.5 36.7 %reduce-scatter.2.cloned.1.call-start = ((), (), s32[]{:S(2)}) async-start(), calls=%async_computation.2 | async-start | bytes 294912 | tf_op jit(solution)/shard_map/reduce_scatter | solution.py:42
  7.4 0.7 copy-start.3
  8.1 0.9 copy-start.1
  10.0 133.3 %all-reduce.2.cloned.1.call-start = ((), (), s32[]{:S(2)}) async-start(), calls=%async_computation.3 | async-start | bytes 2097152 | tf_op jit(solution)/shard_map/psum | solution.py:46
Sparse Core Ops, SparseCore 0:
  10.1 33.0 reduce-scatter.1
  52.6 90.6 all-reduce.1
where the time goes:
time: 162 us
  waiting for transfers between devices  123 us (76%)
  between operations  14.1 us (9%)
  other arithmetic  8.1 us (5%)
  matrix products  7.22 us (4%)
  blocking collectives  7.19 us (4%)
  local copies, waits for them, and re-layouts  1.73 us (1%)
    psum x1, waiting for transfers between devices, shards(): gram = lax.psum(local_gram, ('chan', 'frame', 'sub'))  90.2 us
    reduce_scatter x1, waiting for transfers between devices, shards(): lax.psum_scatter(out, ('chan', 'sub'), scatter_dimension=0, tiled=True)  33.1 us
    all_to_all x1, blocking collectives, shards(): lax.all_to_all(owned, 'frame', split_axis=0, concat_axis=1, tiled=True)  7.19 us
    another operation x3, other arithmetic, clutter_basis(): lower = jnp.linalg.cholesky(matrix)  3.6 us
  transfers between devices with their start and end apart: 2, of which 2 were waited for; matrix products, arithmetic and copies ran while one was open for 0% of the time, Pallas kernels for 0%

commit v1 on v0

v1 whole, which is shorter than its diff:
```python
import functools
import math

import jax
import jax.numpy as jnp
import ml_dtypes
import numpy as np
from jax import lax
from jax.experimental import pallas as pl
from jax.experimental.pallas import tpu as pltpu
from jax.sharding import PartitionSpec as P

RMAX = 32
LANES = 128
SUBL = 8
F32 = jnp.float32
BF16 = jnp.bfloat16
NT = (((1,), (1,)), ((), ()))
NN = (((1,), (0,)), ((), ()))
TN = (((0,), (0,)), ((), ()))


def start_parts(frames):
    at = np.arange(frames, dtype=np.float64)[None, :] + 0.5
    order = np.arange(RMAX, dtype=np.float64)[:, None]
    start = np.cos(math.pi * at * order / frames) * math.sqrt(2.0 / frames)
    high = start.astype(ml_dtypes.bfloat16)
    low = (start - high.astype(np.float64)).astype(ml_dtypes.bfloat16)
    return np.concatenate([high, low], axis=0)


def split(x):
    high = x.astype(BF16)
    return high, (x - high.astype(F32)).astype(BF16)


def mm(a, b, dims):
    return lax.dot_general(a, b, dims, preferred_element_type=F32)


def each(count, body):
    if count <= 16:
        for i in range(count):
            body(i)
    else:
        lax.fori_loop(0, count, lambda i, c: (body(i), c)[1], 0)


def kernel(
    dims,
    index_ref,
    live_ref,
    rank_ref,
    rf_hbm,
    w_hbm,
    start_hbm,
    out_ref,
    rf,
    w,
    start,
    part,
    slots,
    mpart,
    mslots,
    full,
    load_sem,
    send_sem,
    recv_sem,
):
    n_chan, n_sub, n_frame = dims
    n = n_chan * n_sub * n_frame
    num_blocks, num_slots, depth, width = w.shape
    vox = slots.shape[1]
    n_lane = full.shape[0]
    n_row = RMAX // SUBL
    tiles = n_lane * n_row
    stride = n // tiles
    group = lax.axis_index("group")
    me = (lax.axis_index("chan") * n_sub + lax.axis_index("sub")) * n_frame + lax.axis_index("frame")

    def place(d):
        return (group, d // (n_sub * n_frame), lax.rem(d, n_frame), lax.rem(d // n_frame, n_sub))

    def send(src, dst, phase, d):
        return pltpu.make_async_remote_copy(
            src_ref=src,
            dst_ref=dst,
            send_sem=send_sem.at[phase],
            recv_sem=recv_sem.at[phase],
            device_id=place(d),
            device_id_type=pl.DeviceIdType.MESH,
        )

    loads = [
        pltpu.make_async_copy(src, dst, load_sem.at[i])
        for i, (src, dst) in enumerate(((rf_hbm, rf), (w_hbm, w), (start_hbm, start)))
    ]
    for load in loads:
        load.start()

    barrier = pltpu.get_barrier_semaphore()
    each(
        n - 1,
        lambda r: pl.semaphore_signal(
            barrier, inc=1, device_id=place(lax.rem(me + r + 1, n)), device_id_type=pl.DeviceIdType.MESH
        ),
    )
    for load in loads:
        load.wait()

    def beam(b):
        total = None
        for p in range(num_slots):
            term = mm(w[b, p], rf[index_ref[0, b, p]], TN) * live_ref[0, b, p].astype(F32)
            total = term if total is None else total + term
        part[pl.ds(b * width, width), :] = total

    each(num_blocks, beam)
    pl.semaphore_wait(barrier, n - 1)

    def rows_of(d):
        return part.at[pl.ds(pl.multiple_of(d * vox, vox), vox), :]

    def scatter(r):
        d = lax.rem(me + r + 1, n)
        send(rows_of(d), slots.at[me], 0, d).start()

    each(n - 1, scatter)
    slots[me] = rows_of(me)[...]
    send(slots.at[pl.ds(0, n - 1)], slots.at[pl.ds(0, n - 1)], 0, me).wait_recv()

    def gather_frame(q):
        if n <= 16:
            total = slots[q]
            for c in range(1, n // n_frame):
                total = total + slots[c * n_frame + q]
            return total
        return lax.fori_loop(1, n // n_frame, lambda c, t: t + slots[c * n_frame + q], slots[q])

    signal = jnp.concatenate([gather_frame(q) for q in range(n_frame)], axis=1)

    s_high, s_low = split(signal)
    t_high, t_low = start[:RMAX, :], start[RMAX:, :]
    rep_high = jnp.concatenate([s_high] * 4, axis=0)
    rep_low = jnp.concatenate([s_low] * 4, axis=0)
    proj = mm(t_high, rep_high, NT) + mm(t_low, rep_high, NT) + mm(t_high, rep_low, NT)
    p_high = proj.astype(BF16).astype(F32)
    lane = lax.broadcasted_iota(jnp.int32, proj.shape, 1)
    proj = jnp.where(lane < 2 * vox, p_high, proj - p_high).astype(BF16)
    sub_part = mm(proj, jnp.concatenate([s_high, s_low] * 2, axis=0), NN)
    for j in range(n_lane):
        mpart[j] = sub_part[:, j * LANES : (j + 1) * LANES]

    def tile(ref, t):
        return ref.at[t // n_row, pl.ds(pl.multiple_of(lax.rem(t, n_row) * SUBL, SUBL), SUBL), :]

    first = me // stride
    reducer = lax.rem(me, stride) == 0

    def to_reducer(r):
        t = lax.rem(first + r + 1, tiles)
        send(tile(mpart, t), mslots.at[me], 1, t * stride).start()

    each(tiles - 1, to_reducer)
    if stride > 1:
        pl.when(jnp.logical_not(reducer))(lambda: to_reducer(tiles - 1))

    def reduce_tile():
        mslots[me] = tile(mpart, first)[...]
        send(mslots.at[pl.ds(0, n - 1)], mslots.at[pl.ds(0, n - 1)], 1, me).wait_recv()
        if n <= 16:
            total = mslots[0]
            for d in range(1, n):
                total = total + mslots[d]
        else:
            total = lax.fori_loop(1, n, lambda d, t: t + mslots[d], mslots[0])
        tile(full, first)[...] = total

        def spread(r):
            send(tile(full, first), tile(full, first), 2, lax.rem(me + r + 1, n)).start()

        each(n - 1, spread)

    if stride > 1:
        pl.when(reducer)(reduce_tile)
        got = mslots.at[pl.ds(0, tiles)]
        pl.when(jnp.logical_not(reducer))(lambda: send(got, got, 2, me).wait_recv())
    else:
        reduce_tile()
    got = mslots.at[pl.ds(0, tiles - 1)]
    if stride > 1:
        pl.when(reducer)(lambda: send(got, got, 2, me).wait_recv())
    else:
        send(got, got, 2, me).wait_recv()

    kept = lax.broadcasted_iota(jnp.int32, (RMAX, 1), 0) < rank_ref[0]
    sub = jnp.concatenate([full[j] for j in range(n_lane)], axis=1)
    sub = jnp.where(kept, sub, 0.0)
    m_high, m_low = split(sub)
    left_high = jnp.concatenate([m_high, s_high], axis=0)
    left_low = jnp.concatenate([m_low, s_low], axis=0)
    rep_high = jnp.concatenate([m_high] * 4, axis=0)
    rep_low = jnp.concatenate([m_low] * 4, axis=0)
    system = mm(left_high, rep_high, NT) + mm(left_low, rep_high, NT) + mm(left_high, rep_low, NT)
    row = lax.broadcasted_iota(jnp.int32, system.shape, 0)
    order = lax.rem(lax.broadcasted_iota(jnp.int32, system.shape, 1), RMAX)
    system = system + jnp.where((row == order) & (row >= rank_ref[0]), 1.0, 0.0)
    order = order[:1]
    for k in range(RMAX):
        at = k % SUBL
        if k and at == 0:
            system = system[SUBL:, :]
        inverse = 1.0 / system[at : at + 1, k : k + 1]
        here = order == k
        factor = jnp.where(here, -inverse, system[at : at + 1, :] * inverse)
        system = jnp.where(here, 0.0, system) - system[:, k : k + 1] * factor
    coeffs = system[SUBL:, :]
    c_high = coeffs.astype(BF16).astype(F32)
    lane = lax.broadcasted_iota(jnp.int32, coeffs.shape, 1)
    coeffs = jnp.where(lane < 2 * RMAX, c_high, coeffs - c_high).astype(BF16)
    clean = signal - mm(coeffs, jnp.concatenate([m_high, m_low] * 2, axis=0), NN)
    power = jnp.sum(clean * clean, axis=1, keepdims=True) * (1.0 / clean.shape[1])
    diagonal = lax.broadcasted_iota(jnp.int32, (vox, vox), 0) == lax.broadcasted_iota(jnp.int32, (vox, vox), 1)
    out_ref[...] = jnp.sum(jnp.where(diagonal, power, 0.0), axis=0, keepdims=True)[None]

    sent = slots.at[pl.ds(0, n - 1)]
    send(sent, sent, 0, me).wait_send()
    sent = mslots.at[pl.ds(0, tiles - 1)]
    send(sent, sent, 1, me).wait_send()
    if stride > 1:
        pl.when(jnp.logical_not(reducer))(lambda: send(mslots.at[0], mslots.at[0], 1, me).wait_send())
    sent = mslots.at[pl.ds(0, n - 1)]
    if stride > 1:
        pl.when(reducer)(lambda: send(sent, sent, 2, me).wait_send())
    else:
        send(sent, sent, 2, me).wait_send()


def shards(dims, rf, weights, sample_block, live, rank):
    n = math.prod(dims)
    _, num_blocks, num_slots, depth, width = weights.shape
    vox = num_blocks * width // n
    frames = rf.shape[1] * dims[2]
    n_lane = frames // LANES
    blocks = rf.reshape(rf.shape[0] // depth, depth, rf.shape[1])
    smem = pl.BlockSpec(memory_space=pltpu.SMEM)
    hbm = pl.BlockSpec(memory_space=pl.ANY)
    return pl.pallas_call(
        functools.partial(kernel, dims),
        out_shape=jax.ShapeDtypeStruct((1, 1, vox), F32),
        in_specs=[smem, smem, smem, hbm, hbm, hbm],
        out_specs=pl.BlockSpec(memory_space=pltpu.VMEM),
        scratch_shapes=[
            pltpu.VMEM(blocks.shape, BF16),
            pltpu.VMEM(weights.shape[1:], BF16),
            pltpu.VMEM((2 * RMAX, frames), BF16),
            pltpu.VMEM((num_blocks * width, rf.shape[1]), F32),
            pltpu.VMEM((n, vox, rf.shape[1]), F32),
            pltpu.VMEM((n_lane, RMAX, LANES), F32),
            pltpu.VMEM((n, SUBL, LANES), F32),
            pltpu.VMEM((n_lane, RMAX, LANES), F32),
            pltpu.SemaphoreType.DMA((3,)),
            pltpu.SemaphoreType.DMA((3,)),
            pltpu.SemaphoreType.DMA((3,)),
        ],
        compiler_params=pltpu.CompilerParams(
            collective_id=0, has_side_effects=True, vmem_limit_bytes=32 * 1024 * 1024
        ),
        name="power_doppler",
    )(sample_block, live, rank, blocks, weights[0], jnp.asarray(start_parts(frames)))


def solution(mesh):
    dims = (mesh.shape["chan"], mesh.shape["sub"], mesh.shape["frame"])
    return jax.shard_map(
        functools.partial(shards, dims),
        mesh=mesh,
        in_specs=(
            P(("group", "chan", "sub"), "frame"),
            P(("chan", "sub"), None, None, None, None),
            P(("chan", "sub"), None, None),
            P(("chan", "sub"), None, None),
            P("group"),
        ),
        out_specs=P(("group", "chan", "sub"), "frame", None),
        check_vma=False,
    )
```

time: 162 us -> 30.4 us (0.19)
  waiting for transfers between devices: 123 us -> 0 us
  Pallas kernels: 0 us -> 25.4 us
  between operations: 14.1 us -> 0.68 us
  other arithmetic: 8.1 us -> 0 us
  matrix products: 7.22 us -> 0 us
  blocking collectives: 7.19 us -> 0 us
  local copies, waits for them, and re-layouts: 1.73 us -> 4.16 us
    psum x1 -> x0, waiting for transfers between devices: 90.2 us -> none  [shards(): gram = lax.psum(local_gram, ('chan', 'frame', 'sub'))]
    reduce_scatter x1 -> x0, waiting for transfers between devices: 33.1 us -> none  [shards(): lax.psum_scatter(out, ('chan', 'sub'), scatter_dimension=0, tiled=True)]
    pallas_call x0 -> x1, Pallas kernels: none -> 25.4 us  [shards(): pl.pallas_call(functools.partial(kernel, dims), out_shape=jax.ShapeDtypeS...]
    all_to_all x1 -> x0, blocking collectives: 7.19 us -> none  [shards(): lax.all_to_all(owned, 'frame', split_axis=0, concat_axis=1, tiled=True)]
    dot_general x6 -> x0, matrix products: 6.94 us -> none  [the longest x1 3.23 us: shards(): subspace = jnp.dot(gram, start, precision=lax.Precision.HIGHEST)]
    another operation x5 -> x0, other arithmetic: 6.68 us -> none  [the longest x3 3.6 us: clutter_basis(): lower = jnp.linalg.cholesky(matrix)]
    unnamed x8 -> x11, local copies, waits for them, and re-layouts: 1.01 us -> 4.16 us
  transfers between devices with their start and end apart: 2 -> 0, of which waited for: 2 -> 0; matrix products, arithmetic and copies ran while one was open for 0% -> 0% of each run, Pallas kernels for 0% -> 0%
where the time goes in v1:
time: 30.4 us; the launch traced here: 30.2 us
  Pallas kernels  25.4 us (84%)
  local copies, waits for them, and re-layouts  4.16 us (14%)
  between operations  0.68 us (2%)
    pallas_call x1, Pallas kernels, shards(): pl.pallas_call(functools.partial(kernel, dims), out_shape=jax.ShapeDtypeS...  25.4 us
    unnamed x11, local copies, waits for them, and re-layouts  4.16 us

profile of v1, /device:TPU:0, one launch (start us, length us, event | category | flops | bytes accessed | tf_op | source)
XLA Modules:
  0.0 30.2 jit_solution(2212632119075087015)
XLA Ops:
  0.7 0.0 copy-start.4
  0.7 0.0 copy-start.3
  0.7 0.7 %copy-done.4 = s32[1,2,2]{2,1,0:T(2,128)S(1)} copy-done((s32[1,2,2]{2,1,0:T(2,128)S(1)}, s32[1,2,2]{2,1,0:T(2,128)}, u32[]{:S(2)}) %copy-start.4) | copy-done | bytes 40
  1.3 0.0 copy-done.3
  1.3 0.0 copy-start
  1.4 1.2 %copy-done = bf16[2048,256]{1,0:T(8,128)(2,1)S(1)} copy-done((bf16[2048,256]{1,0:T(8,128)(2,1)S(1)}, bf16[2048,256]{1,0:T(8,128)(2,1)}, u32[]{:S(2)}) %copy-start) | copy-done | bytes 1048600
  2.6 0.0 copy-start.1
  2.6 0.9 %copy-done.1 = bf16[1,2,2,128,128]{4,3,2,1,0:T(8,128)(2,1)S(1)} copy-done((bf16[1,2,2,128,128]{4,3,2,1,0:T(8,128)(2,1)S(1)}, bf16[1,2,2,128,128]{4,3,2,1,0:T(8,128)(2,1)}, u32[]{:S(2)}) %copy-start.1) | copy-done | bytes 131096
  3.5 0.0 copy-start.2
  3.5 0.8 %copy-done.2 = bf16[64,512]{1,0:T(8,128)(2,1)S(1)} copy-done((bf16[64,512]{1,0:T(8,128)(2,1)S(1)}, bf16[64,512]{1,0:T(8,128)(2,1)}, u32[]{:S(2)}) %copy-start.2) | copy-done | bytes 65560
  4.3 25.4 %power_doppler.1 = f32[1,1,16]{2,1,0:T(1,128)S(1)} custom-call(s32[1,2,2]{2,1,0:T(2,128)S(1)} %copy-done.3, s32[1,2,2]{2,1,0:T(2,128)S(1)} %copy-done.4, s32[1]{0:T(128)S(6)} %copy.8.rank_ref, bf16[16,128,256]{2,1,0:T(8,128)(2,1)S(1)} %bitcast.2, bf16[2,2,128,128]{3,2,1,0:T(8,128)(2,1)S(1)} %bitcast.3, bf16[64,512]{1,0:T(8,128)(2,1)S(1)} %copy-done.2), custom_call_target="tpu_custom_call" | custom-call | tf_op jit(solution)/shard_map/power_doppler/pallas_call | solution.py:248
  29.7 0.5 %copy.9 = f32[1,1,16]{2,1,0:T(1,128)} copy(f32[1,1,16]{2,1,0:T(1,128)S(1)} %power_doppler.1) | data formatting | bytes 128
Async XLA Ops:
  0.7 0.7 %copy-start.4 = (s32[1,2,2]{2,1,0:T(2,128)S(1)}, s32[1,2,2]{2,1,0:T(2,128)}, u32[]{:S(2)}) copy-start(s32[1,2,2]{2,1,0:T(2,128)} %live_ref.1) | copy-start | bytes 52
  0.7 0.7 %copy-start.3 = (s32[1,2,2]{2,1,0:T(2,128)S(1)}, s32[1,2,2]{2,1,0:T(2,128)}, u32[]{:S(2)}) copy-start(s32[1,2,2]{2,1,0:T(2,128)} %index_ref.1) | copy-start | bytes 52
  1.3 1.2 %copy-start = (bf16[2048,256]{1,0:T(8,128)(2,1)S(1)}, bf16[2048,256]{1,0:T(8,128)(2,1)}, u32[]{:S(2)}) copy-start(bf16[2048,256]{1,0:T(8,128)(2,1)} %param.6) | copy-start | bytes 3145732
  2.6 0.9 %copy-start.1 = (bf16[1,2,2,128,128]{4,3,2,1,0:T(8,128)(2,1)S(1)}, bf16[1,2,2,128,128]{4,3,2,1,0:T(8,128)(2,1)}, u32[]{:S(2)}) copy-start(bf16[1,2,2,128,128]{4,3,2,1,0:T(8,128)(2,1)} %param.7) | copy-start | bytes 393220
  3.5 0.8 %copy-start.2 = (bf16[64,512]{1,0:T(8,128)(2,1)S(1)}, bf16[64,512]{1,0:T(8,128)(2,1)}, u32[]{:S(2)}) copy-start(bf16[64,512]{1,0:T(8,128)(2,1)} %constant.2.clone.start_hbm) | copy-start | bytes 196612

commit v2 on v1

--- a/solution.py
+++ b/solution.py
@@ -3,7 +3,6 @@
 
 import jax
 import jax.numpy as jnp
-import ml_dtypes
 import numpy as np
 from jax import lax
 from jax.experimental import pallas as pl
@@ -13,6 +12,7 @@
 RMAX = 32
 LANES = 128
 SUBL = 8
+UNIT = 16
 F32 = jnp.float32
 BF16 = jnp.bfloat16
 NT = (((1,), (1,)), ((), ()))
@@ -20,13 +20,10 @@
 TN = (((0,), (0,)), ((), ()))
 
 
-def start_parts(frames):
+def start_basis(frames):
     at = np.arange(frames, dtype=np.float64)[None, :] + 0.5
     order = np.arange(RMAX, dtype=np.float64)[:, None]
-    start = np.cos(math.pi * at * order / frames) * math.sqrt(2.0 / frames)
-    high = start.astype(ml_dtypes.bfloat16)
-    low = (start - high.astype(np.float64)).astype(ml_dtypes.bfloat16)
-    return np.concatenate([high, low], axis=0)
+    return (np.cos(math.pi * at * order / frames) * math.sqrt(2.0 / frames)).astype(np.float32)
 
 
 def split(x):
@@ -48,13 +45,16 @@
 
 def kernel(
     dims,
-    index_ref,
-    live_ref,
-    rank_ref,
+    index_hbm,
+    live_hbm,
+    rank_hbm,
     rf_hbm,
     w_hbm,
     start_hbm,
     out_ref,
+    index_ref,
+    live_ref,
+    rank_ref,
     rf,
     w,
     start,
@@ -72,11 +72,18 @@
     num_blocks, num_slots, depth, width = w.shape
     vox = slots.shape[1]
     n_lane = full.shape[0]
-    n_row = RMAX // SUBL
-    tiles = n_lane * n_row
-    stride = n // tiles
     group = lax.axis_index("group")
     me = (lax.axis_index("chan") * n_sub + lax.axis_index("sub")) * n_frame + lax.axis_index("frame")
+
+    def partner(r):
+        if not isinstance(r, int):
+            return lax.rem(me + r, n)
+        d, bit = me, 1
+        while bit <= r:
+            if r & bit:
+                d = d + bit - 2 * bit * lax.rem(me // bit, 2)
+            bit *= 2
+        return d
 
     def place(d):
         return (group, d // (n_sub * n_frame), lax.rem(d, n_frame), lax.rem(d // n_frame, n_sub))
@@ -93,7 +100,16 @@
 
     loads = [
         pltpu.make_async_copy(src, dst, load_sem.at[i])
-        for i, (src, dst) in enumerate(((rf_hbm, rf), (w_hbm, w), (start_hbm, start)))
+        for i, (src, dst) in enumerate(
+            (
+                (index_hbm, index_ref),
+                (live_hbm, live_ref),
+                (rank_hbm, rank_ref),
+                (rf_hbm, rf),
+                (w_hbm, w),
+                (start_hbm, start),
+            )
+        )
     ]
     for load in loads:
         load.start()
@@ -102,7 +118,7 @@
     each(
         n - 1,
         lambda r: pl.semaphore_signal(
-            barrier, inc=1, device_id=place(lax.rem(me + r + 1, n)), device_id_type=pl.DeviceIdType.MESH
+            barrier, inc=1, device_id=place(partner(n - 1 - r)), device_id_type=pl.DeviceIdType.MESH
         ),
     )
     for load in loads:
@@ -122,7 +138,7 @@
         return part.at[pl.ds(pl.multiple_of(d * vox, vox), vox), :]
 
     def scatter(r):
-        d = lax.rem(me + r + 1, n)
+        d = partner(n - 1 - r)
         send(rows_of(d), slots.at[me], 0, d).start()
 
     each(n - 1, scatter)
@@ -140,7 +156,7 @@
     signal = jnp.concatenate([gather_frame(q) for q in range(n_frame)], axis=1)
 
     s_high, s_low = split(signal)
-    t_high, t_low = start[:RMAX, :], start[RMAX:, :]
+    t_high, t_low = split(start[...])
     rep_high = jnp.concatenate([s_high] * 4, axis=0)
     rep_low = jnp.concatenate([s_low] * 4, axis=0)
     proj = mm(t_high, rep_high, NT) + mm(t_low, rep_high, NT) + mm(t_high, rep_low, NT)
@@ -151,22 +167,28 @@
     for j in range(n_lane):
         mpart[j] = sub_part[:, j * LANES : (j + 1) * LANES]
 
-    def tile(ref, t):
-        return ref.at[t // n_row, pl.ds(pl.multiple_of(lax.rem(t, n_row) * SUBL, SUBL), SUBL), :]
-
-    first = me // stride
-    reducer = lax.rem(me, stride) == 0
+    base = (n_chan // 2 - 1) * n_sub * n_frame
+    units = n_lane * (RMAX // UNIT)
+    reducer = (me >= base) & (me < base + units)
+
+    def unit(ref, u):
+        return ref.at[u // (RMAX // UNIT), pl.ds(pl.multiple_of(lax.rem(u, RMAX // UNIT) * UNIT, UNIT), UNIT), :]
+
+    far = jnp.where(me < n // 2, units // 2, 0)
 
     def to_reducer(r):
-        t = lax.rem(first + r + 1, tiles)
-        send(tile(mpart, t), mslots.at[me], 1, t * stride).start()
-
-    each(tiles - 1, to_reducer)
-    if stride > 1:
-        pl.when(jnp.logical_not(reducer))(lambda: to_reducer(tiles - 1))
-
-    def reduce_tile():
-        mslots[me] = tile(mpart, first)[...]
+        u = lax.rem(far + r, units)
+
+        @pl.when(base + u != me)
+        def _():
+            send(unit(mpart, u), mslots.at[me], 1, base + u).start()
+
+    each(units, to_reducer)
+
+    @pl.when(reducer)
+    def _():
+        mine = me - base
+        mslots[me] = unit(mpart, mine)[...]
         send(mslots.at[pl.ds(0, n - 1)], mslots.at[pl.ds(0, n - 1)], 1, me).wait_recv()
         if n <= 16:
             total = mslots[0]
@@ -174,26 +196,17 @@
                 total = total + mslots[d]
         else:
             total = lax.fori_loop(1, n, lambda d, t: t + mslots[d], mslots[0])
-        tile(full, first)[...] = total
-
-        def spread(r):
-            send(tile(full, first), tile(full, first), 2, lax.rem(me + r + 1, n)).start()
-
-        each(n - 1, spread)
-
-    if stride > 1:
-        pl.when(reducer)(reduce_tile)
-        got = mslots.at[pl.ds(0, tiles)]
-        pl.when(jnp.logical_not(reducer))(lambda: send(got, got, 2, me).wait_recv())
-    else:
-        reduce_tile()
-    got = mslots.at[pl.ds(0, tiles - 1)]
-    if stride > 1:
-        pl.when(reducer)(lambda: send(got, got, 2, me).wait_recv())
-    else:
+        unit(full, mine)[...] = total
+        each(n - 1, lambda r: send(unit(full, mine), unit(full, mine), 2, partner(n - 1 - r)).start())
+        got = mslots.at[pl.ds(0, units - 1)]
         send(got, got, 2, me).wait_recv()
 
-    kept = lax.broadcasted_iota(jnp.int32, (RMAX, 1), 0) < rank_ref[0]
+    @pl.when(jnp.logical_not(reducer))
+    def _():
+        got = mslots.at[pl.ds(0, units)]
+        send(got, got, 2, me).wait_recv()
+
+    kept = lax.broadcasted_iota(jnp.int32, (RMAX, 1), 0) < rank_ref[0, 0]
     sub = jnp.concatenate([full[j] for j in range(n_lane)], axis=1)
     sub = jnp.where(kept, sub, 0.0)
     m_high, m_low = split(sub)
@@ -204,7 +217,7 @@
     system = mm(left_high, rep_high, NT) + mm(left_low, rep_high, NT) + mm(left_high, rep_low, NT)
     row = lax.broadcasted_iota(jnp.int32, system.shape, 0)
     order = lax.rem(lax.broadcasted_iota(jnp.int32, system.shape, 1), RMAX)
-    system = system + jnp.where((row == order) & (row >= rank_ref[0]), 1.0, 0.0)
+    system = system + jnp.where((row == order) & (row >= rank_ref[0, 0]), 1.0, 0.0)
     order = order[:1]
     for k in range(RMAX):
         at = k % SUBL
@@ -225,15 +238,18 @@
 
     sent = slots.at[pl.ds(0, n - 1)]
     send(sent, sent, 0, me).wait_send()
-    sent = mslots.at[pl.ds(0, tiles - 1)]
-    send(sent, sent, 1, me).wait_send()
-    if stride > 1:
-        pl.when(jnp.logical_not(reducer))(lambda: send(mslots.at[0], mslots.at[0], 1, me).wait_send())
-    sent = mslots.at[pl.ds(0, n - 1)]
-    if stride > 1:
-        pl.when(reducer)(lambda: send(sent, sent, 2, me).wait_send())
-    else:
+
+    @pl.when(reducer)
+    def _():
+        sent = mslots.at[pl.ds(0, units - 1)]
+        send(sent, sent, 1, me).wait_send()
+        sent = mslots.at[pl.ds(0, n - 1)]
         send(sent, sent, 2, me).wait_send()
+
+    @pl.when(jnp.logical_not(reducer))
+    def _():
+        sent = mslots.at[pl.ds(0, units)]
+        send(sent, sent, 1, me).wait_send()
 
 
 def shards(dims, rf, weights, sample_block, live, rank):
@@ -242,32 +258,35 @@
     vox = num_blocks * width // n
     frames = rf.shape[1] * dims[2]
     n_lane = frames // LANES
+    rank = rank[None]
     blocks = rf.reshape(rf.shape[0] // depth, depth, rf.shape[1])
-    smem = pl.BlockSpec(memory_space=pltpu.SMEM)
     hbm = pl.BlockSpec(memory_space=pl.ANY)
     return pl.pallas_call(
         functools.partial(kernel, dims),
         out_shape=jax.ShapeDtypeStruct((1, 1, vox), F32),
-        in_specs=[smem, smem, smem, hbm, hbm, hbm],
+        in_specs=[hbm] * 6,
         out_specs=pl.BlockSpec(memory_space=pltpu.VMEM),
         scratch_shapes=[
+            pltpu.SMEM(sample_block.shape, jnp.int32),
+            pltpu.SMEM(live.shape, jnp.int32),
+            pltpu.SMEM(rank.shape, jnp.int32),
             pltpu.VMEM(blocks.shape, BF16),
             pltpu.VMEM(weights.shape[1:], BF16),
-            pltpu.VMEM((2 * RMAX, frames), BF16),
+            pltpu.VMEM((RMAX, frames), F32),
             pltpu.VMEM((num_blocks * width, rf.shape[1]), F32),
             pltpu.VMEM((n, vox, rf.shape[1]), F32),
             pltpu.VMEM((n_lane, RMAX, LANES), F32),
-            pltpu.VMEM((n, SUBL, LANES), F32),
+            pltpu.VMEM((n, UNIT, LANES), F32),
             pltpu.VMEM((n_lane, RMAX, LANES), F32),
-            pltpu.SemaphoreType.DMA((3,)),
+            pltpu.SemaphoreType.DMA((6,)),
             pltpu.SemaphoreType.DMA((3,)),
             pltpu.SemaphoreType.DMA((3,)),
         ],
         compiler_params=pltpu.CompilerParams(
-            collective_id=0, has_side_effects=True, vmem_limit_bytes=32 * 1024 * 1024
+            collective_id=0, has_side_effects=True, vmem_limit_bytes=60 * 1024 * 1024
         ),
         name="power_doppler",
-    )(sample_block, live, rank, blocks, weights[0], jnp.asarray(start_parts(frames)))
+    )(sample_block, live, rank, blocks, weights[0], jnp.asarray(start_basis(frames)))
 
 
 def solution(mesh):

time: 30.4 us -> 27.8 us (0.914)
  local copies, waits for them, and re-layouts: 4.16 us -> 1.19 us
  Pallas kernels: 25.4 us -> 25.8 us
    unnamed x11 -> x1, local copies, waits for them, and re-layouts: 4.16 us -> 1.19 us
    pallas_call x1, Pallas kernels: 25.4 us -> 25.8 us  [shards(): pl.pallas_call(functools.partial(kernel, dims), out_shape=jax.ShapeDtypeS...]
where the time goes in v2:
time: 27.8 us; the launch traced here: 27.6 us
  Pallas kernels  25.8 us (93%)
  local copies, waits for them, and re-layouts  1.19 us (4%)
  between operations  0.66 us (2%)
    pallas_call x1, Pallas kernels, shards(): pl.pallas_call(functools.partial(kernel, dims), out_shape=jax.ShapeDtypeS...  25.8 us
    unnamed x1, local copies, waits for them, and re-layouts  1.19 us

profile of v2, /device:TPU:0, one launch (start us, length us, event | category | flops | bytes accessed | tf_op | source)
XLA Modules:
  0.0 27.6 jit_solution(3991086194139947016)
XLA Ops:
  0.7 25.8 %power_doppler.1 = f32[1,1,16]{2,1,0:T(1,128)} custom-call(s32[1,2,2]{2,1,0:T(2,128)} %index_hbm.1, s32[1,2,2]{2,1,0:T(2,128)} %live_hbm.1, s32[1,1]{1,0:T(1,128)} %bitcast.3.rank_hbm, bf16[16,128,256]{2,1,0:T(8,128)(2,1)} %bitcast.4, bf16[2,2,128,128]{3,2,1,0:T(8,128)(2,1)} %bitcast.5, f32[32,512]{1,0:T(8,128)} %constant.2.clone.start_hbm), custom_call_target="tpu_custom_call" | custom-call | tf_op jit(solution)/shard_map/power_doppler/pallas_call | solution.py:264
  26.4 1.2 %copy.9 = f32[1,1,16]{2,1,0:T(1,128)} copy(f32[1,1,16]{2,1,0:T(1,128)} %power_doppler.1) | data formatting | bytes 128

commit v3 on v2

--- a/solution.py
+++ b/solution.py
@@ -208,7 +208,8 @@
 
     kept = lax.broadcasted_iota(jnp.int32, (RMAX, 1), 0) < rank_ref[0, 0]
     sub = jnp.concatenate([full[j] for j in range(n_lane)], axis=1)
-    sub = jnp.where(kept, sub, 0.0)
+    norm = jnp.sum(sub * sub, axis=1, keepdims=True)
+    sub = jnp.where(kept, sub * lax.rsqrt(norm), 0.0)
     m_high, m_low = split(sub)
     left_high = jnp.concatenate([m_high, s_high], axis=0)
     left_low = jnp.concatenate([m_low, s_low], axis=0)
@@ -219,14 +220,20 @@
     order = lax.rem(lax.broadcasted_iota(jnp.int32, system.shape, 1), RMAX)
     system = system + jnp.where((row == order) & (row >= rank_ref[0, 0]), 1.0, 0.0)
     order = order[:1]
-    for k in range(RMAX):
+    for k in range(0, RMAX, 2):
         at = k % SUBL
         if k and at == 0:
             system = system[SUBL:, :]
-        inverse = 1.0 / system[at : at + 1, k : k + 1]
-        here = order == k
-        factor = jnp.where(here, -inverse, system[at : at + 1, :] * inverse)
-        system = jnp.where(here, 0.0, system) - system[:, k : k + 1] * factor
+        column0 = jnp.broadcast_to(system[:, k : k + 1], system.shape)
+        column1 = jnp.broadcast_to(system[:, k + 1 : k + 2], system.shape)
+        here0, here1 = order == k, order == k + 1
+        row0 = jnp.where(here0, -1.0, jnp.where(here1, 0.0, system[at : at + 1, :]))
+        row1 = jnp.where(here0, 0.0, jnp.where(here1, -1.0, system[at + 1 : at + 2, :]))
+        p00, p01, p11 = column0[at : at + 1, :], column1[at : at + 1, :], column1[at + 1 : at + 2, :]
+        inverse = 1.0 / (p00 * p11 - p01 * p01)
+        factor0 = (p11 * row0 - p01 * row1) * inverse
+        factor1 = (p00 * row1 - p01 * row0) * inverse
+        system = jnp.where(here0 | here1, 0.0, system) - column0 * factor0 - column1 * factor1
     coeffs = system[SUBL:, :]
     c_high = coeffs.astype(BF16).astype(F32)
     lane = lax.broadcasted_iota(jnp.int32, coeffs.shape, 1)
@@ -263,7 +270,7 @@
     hbm = pl.BlockSpec(memory_space=pl.ANY)
     return pl.pallas_call(
         functools.partial(kernel, dims),
-        out_shape=jax.ShapeDtypeStruct((1, 1, vox), F32),
+        out_shape=pltpu.VMEM((1, 1, vox), F32),
         in_specs=[hbm] * 6,
         out_specs=pl.BlockSpec(memory_space=pltpu.VMEM),
         scratch_shapes=[

time: 27.8 us -> 25.3 us (0.910)
  Pallas kernels: 25.8 us -> 24 us
  local copies, waits for them, and re-layouts: 1.19 us -> 0.51 us
    pallas_call x1, Pallas kernels: 25.8 us -> 24 us  [shards(): pl.pallas_call(functools.partial(kernel, dims), out_shape=pltpu.VMEM((1,...]
    unnamed x1, local copies, waits for them, and re-layouts: 1.19 us -> 0.51 us
where the time goes in v3:
time: 25.3 us; the launch traced here: 25.2 us
  Pallas kernels  24 us (95%)
  between operations  0.66 us (3%)
  local copies, waits for them, and re-layouts  0.51 us (2%)
    pallas_call x1, Pallas kernels, shards(): pl.pallas_call(functools.partial(kernel, dims), out_shape=pltpu.VMEM((1,...  24 us
    unnamed x1, local copies, waits for them, and re-layouts  0.51 us

profile of v3, /device:TPU:0, one launch (start us, length us, event | category | flops | bytes accessed | tf_op | source)
XLA Modules:
  0.0 25.2 jit_solution(6613227949088532925)
XLA Ops:
  0.7 24.0 %power_doppler.1 = f32[1,1,16]{2,1,0:T(1,128)S(1)} custom-call(s32[1,2,2]{2,1,0:T(2,128)} %index_hbm.1, s32[1,2,2]{2,1,0:T(2,128)} %live_hbm.1, s32[1,1]{1,0:T(1,128)} %bitcast.3.rank_hbm, bf16[16,128,256]{2,1,0:T(8,128)(2,1)} %bitcast.4, bf16[2,2,128,128]{3,2,1,0:T(8,128)(2,1)} %bitcast.5, f32[32,512]{1,0:T(8,128)} %constant.2.clone.start_hbm), custom_call_target="tpu_custom_call" | custom-call | tf_op jit(solution)/shard_map/power_doppler/pallas_call | solution.py:271
  24.7 0.5 %copy.8 = f32[1,1,16]{2,1,0:T(1,128)} copy(f32[1,1,16]{2,1,0:T(1,128)S(1)} %power_doppler.1) | data formatting | bytes 128

commit v4 on v3

--- a/solution.py
+++ b/solution.py
@@ -59,6 +59,8 @@
     w,
     start,
     part,
+    pair,
+    sums,
     slots,
     mpart,
     mslots,
@@ -66,6 +68,8 @@
     load_sem,
     send_sem,
     recv_sem,
+    pair_send,
+    pair_recv,
 ):
     n_chan, n_sub, n_frame = dims
     n = n_chan * n_sub * n_frame
@@ -134,24 +138,70 @@
     each(num_blocks, beam)
     pl.semaphore_wait(barrier, n - 1)
 
-    def rows_of(d):
-        return part.at[pl.ds(pl.multiple_of(d * vox, vox), vox), :]
+    sub, frame = lax.axis_index("sub"), lax.axis_index("frame")
+    chan = lax.axis_index("chan")
+    span = n_frame * vox
+
+    def rows(c, s):
+        return pl.ds(pl.multiple_of((c * n_sub + s) * span, span), span)
+
+    def nth_chan(r):
+        if n_chan <= 4:
+            c, bit = chan, 1
+            flip = n_chan - 1 - r
+            while bit <= flip:
+                if flip & bit:
+                    c = c + bit - 2 * bit * lax.rem(chan // bit, 2)
+                bit *= 2
+            return c
+        return lax.rem(chan + r + 1, n_chan)
+
+    def exchange(r):
+        c = nth_chan(r)
+        return pltpu.make_async_remote_copy(
+            src_ref=part.at[rows(c, 1 - sub), :],
+            dst_ref=pair.at[r],
+            send_sem=pair_send.at[r],
+            recv_sem=pair_recv.at[r],
+            device_id=(group, chan, frame, 1 - sub),
+            device_id_type=pl.DeviceIdType.MESH,
+        )
+
+    each(n_chan, lambda r: exchange(r).start())
+    mine = chan * n_frame + frame
 
     def scatter(r):
-        d = partner(n - 1 - r)
-        send(rows_of(d), slots.at[me], 0, d).start()
-
-    each(n - 1, scatter)
-    slots[me] = rows_of(me)[...]
-    send(slots.at[pl.ds(0, n - 1)], slots.at[pl.ds(0, n - 1)], 0, me).wait_recv()
+        c = nth_chan(r)
+        exchange(r).wait_recv()
+        sums[r] = pair[r] + part[rows(c, sub), :]
+        for step in range(n_frame):
+            q = lax.rem(frame + n_frame - 1 - step, n_frame)
+            source = sums.at[r, pl.ds(pl.multiple_of(q * vox, vox), vox), :]
+
+            def go():
+                send(source, slots.at[mine], 0, (c * n_sub + sub) * n_frame + q).start()
+
+            if n_chan <= 4 and r < n_chan - 1 or step < n_frame - 1:
+                go()
+            elif n_chan <= 4:
+                slots[mine] = source[...]
+            else:
+                pl.when(r < n_chan - 1)(go)
+
+    each(n_chan, scatter)
+    if n_chan > 4:
+        slots[mine] = sums[n_chan - 1, pl.ds(pl.multiple_of(frame * vox, vox), vox), :]
+    peers = n_chan * n_frame
+    got = slots.at[pl.ds(0, peers - 1)]
+    send(got, got, 0, me).wait_recv()
 
     def gather_frame(q):
         if n <= 16:
             total = slots[q]
-            for c in range(1, n // n_frame):
+            for c in range(1, n_chan):
                 total = total + slots[c * n_frame + q]
             return total
-        return lax.fori_loop(1, n // n_frame, lambda c, t: t + slots[c * n_frame + q], slots[q])
+        return lax.fori_loop(1, n_chan, lambda c, t: t + slots[c * n_frame + q], slots[q])
 
     signal = jnp.concatenate([gather_frame(q) for q in range(n_frame)], axis=1)
 
@@ -207,10 +257,10 @@
         send(got, got, 2, me).wait_recv()
 
     kept = lax.broadcasted_iota(jnp.int32, (RMAX, 1), 0) < rank_ref[0, 0]
-    sub = jnp.concatenate([full[j] for j in range(n_lane)], axis=1)
-    norm = jnp.sum(sub * sub, axis=1, keepdims=True)
-    sub = jnp.where(kept, sub * lax.rsqrt(norm), 0.0)
-    m_high, m_low = split(sub)
+    space = jnp.concatenate([full[j] for j in range(n_lane)], axis=1)
+    norm = jnp.sum(space * space, axis=1, keepdims=True)
+    space = jnp.where(kept, space * lax.rsqrt(norm), 0.0)
+    m_high, m_low = split(space)
     left_high = jnp.concatenate([m_high, s_high], axis=0)
     left_low = jnp.concatenate([m_low, s_low], axis=0)
     rep_high = jnp.concatenate([m_high] * 4, axis=0)
@@ -243,8 +293,9 @@
     diagonal = lax.broadcasted_iota(jnp.int32, (vox, vox), 0) == lax.broadcasted_iota(jnp.int32, (vox, vox), 1)
     out_ref[...] = jnp.sum(jnp.where(diagonal, power, 0.0), axis=0, keepdims=True)[None]
 
-    sent = slots.at[pl.ds(0, n - 1)]
+    sent = slots.at[pl.ds(0, peers - 1)]
     send(sent, sent, 0, me).wait_send()
+    each(n_chan, lambda r: exchange(r).wait_send())
 
     @pl.when(reducer)
     def _():
@@ -281,13 +332,17 @@
             pltpu.VMEM(weights.shape[1:], BF16),
             pltpu.VMEM((RMAX, frames), F32),
             pltpu.VMEM((num_blocks * width, rf.shape[1]), F32),
-            pltpu.VMEM((n, vox, rf.shape[1]), F32),
+            pltpu.VMEM((dims[0], dims[2] * vox, rf.shape[1]), F32),
+            pltpu.VMEM((dims[0], dims[2] * vox, rf.shape[1]), F32),
+            pltpu.VMEM((dims[0] * dims[2], vox, rf.shape[1]), F32),
             pltpu.VMEM((n_lane, RMAX, LANES), F32),
             pltpu.VMEM((n, UNIT, LANES), F32),
             pltpu.VMEM((n_lane, RMAX, LANES), F32),
             pltpu.SemaphoreType.DMA((6,)),
             pltpu.SemaphoreType.DMA((3,)),
             pltpu.SemaphoreType.DMA((3,)),
+            pltpu.SemaphoreType.DMA((dims[0],)),
+            pltpu.SemaphoreType.DMA((dims[0],)),
         ],
         compiler_params=pltpu.CompilerParams(
             collective_id=0, has_side_effects=True, vmem_limit_bytes=60 * 1024 * 1024

time: 25.3 us -> 23.8 us (0.941)
  Pallas kernels: 24 us -> 22.4 us
    pallas_call x1, Pallas kernels: 24 us -> 22.4 us  [shards(): pl.pallas_call(functools.partial(kernel, dims), out_shape=pltpu.VMEM((1,...]
where the time goes in v4:
time: 23.8 us; the launch traced here: 23.6 us
  Pallas kernels  22.4 us (94%)
  between operations  0.66 us (3%)
  local copies, waits for them, and re-layouts  0.51 us (2%)
    pallas_call x1, Pallas kernels, shards(): pl.pallas_call(functools.partial(kernel, dims), out_shape=pltpu.VMEM((1,...  22.4 us
    unnamed x1, local copies, waits for them, and re-layouts  0.51 us

profile of v4, /device:TPU:0, one launch (start us, length us, event | category | flops | bytes accessed | tf_op | source)
XLA Modules:
  0.0 23.6 jit_solution(10254568203768837434)
XLA Ops:
  0.7 22.4 %power_doppler.1 = f32[1,1,16]{2,1,0:T(1,128)S(1)} custom-call(s32[1,2,2]{2,1,0:T(2,128)} %index_hbm.1, s32[1,2,2]{2,1,0:T(2,128)} %live_hbm.1, s32[1,1]{1,0:T(1,128)} %bitcast.3.rank_hbm, bf16[16,128,256]{2,1,0:T(8,128)(2,1)} %bitcast.4, bf16[2,2,128,128]{3,2,1,0:T(8,128)(2,1)} %bitcast.5, f32[32,512]{1,0:T(8,128)} %constant.2.clone.start_hbm), custom_call_target="tpu_custom_call" | custom-call | tf_op jit(solution)/shard_map/power_doppler/pallas_call | solution.py:322
  23.1 0.5 %copy.8 = f32[1,1,16]{2,1,0:T(1,128)} copy(f32[1,1,16]{2,1,0:T(1,128)S(1)} %power_doppler.1) | data formatting | bytes 128

commit v5 on v4

--- a/solution.py
+++ b/solution.py
@@ -115,9 +115,6 @@
             )
         )
     ]
-    for load in loads:
-        load.start()
-
     barrier = pltpu.get_barrier_semaphore()
     each(
         n - 1,
@@ -125,6 +122,8 @@
             barrier, inc=1, device_id=place(partner(n - 1 - r)), device_id_type=pl.DeviceIdType.MESH
         ),
     )
+    for load in loads:
+        load.start()
     for load in loads:
         load.wait()
 
@@ -270,20 +269,26 @@
     order = lax.rem(lax.broadcasted_iota(jnp.int32, system.shape, 1), RMAX)
     system = system + jnp.where((row == order) & (row >= rank_ref[0, 0]), 1.0, 0.0)
     order = order[:1]
-    for k in range(0, RMAX, 2):
-        at = k % SUBL
-        if k and at == 0:
+    for panel in range(0, RMAX, SUBL):
+        if panel:
             system = system[SUBL:, :]
-        column0 = jnp.broadcast_to(system[:, k : k + 1], system.shape)
-        column1 = jnp.broadcast_to(system[:, k + 1 : k + 2], system.shape)
-        here0, here1 = order == k, order == k + 1
-        row0 = jnp.where(here0, -1.0, jnp.where(here1, 0.0, system[at : at + 1, :]))
-        row1 = jnp.where(here0, 0.0, jnp.where(here1, -1.0, system[at + 1 : at + 2, :]))
-        p00, p01, p11 = column0[at : at + 1, :], column1[at : at + 1, :], column1[at + 1 : at + 2, :]
-        inverse = 1.0 / (p00 * p11 - p01 * p01)
-        factor0 = (p11 * row0 - p01 * row1) * inverse
-        factor1 = (p00 * row1 - p01 * row0) * inverse
-        system = jnp.where(here0 | here1, 0.0, system) - column0 * factor0 - column1 * factor1
+        columns = [jnp.broadcast_to(system[:, panel + i : panel + i + 1], system.shape) for i in range(SUBL)]
+        for i in range(0, SUBL, 2):
+            column0, column1 = columns[i : i + 2]
+            p00, p01, p11 = column0[i : i + 1, :], column1[i : i + 1, :], column1[i + 1 : i + 2, :]
+            inverse = 1.0 / (p00 * p11 - p01 * p01)
+
+            def update(target, row0, row1):
+                factor0 = (p11 * row0 - p01 * row1) * inverse
+                factor1 = (p00 * row1 - p01 * row0) * inverse
+                return target - column0 * factor0 - column1 * factor1
+
+            for j in range(i + 2, SUBL):
+                columns[j] = update(columns[j], columns[j][i : i + 1, :], columns[j][i + 1 : i + 2, :])
+            here0, here1 = order == panel + i, order == panel + i + 1
+            row0 = jnp.where(here0, -1.0, jnp.where(here1, 0.0, system[i : i + 1, :]))
+            row1 = jnp.where(here0, 0.0, jnp.where(here1, -1.0, system[i + 1 : i + 2, :]))
+            system = update(jnp.where(here0 | here1, 0.0, system), row0, row1)
     coeffs = system[SUBL:, :]
     c_high = coeffs.astype(BF16).astype(F32)
     lane = lax.broadcasted_iota(jnp.int32, coeffs.shape, 1)

time: 23.8 us -> 23 us (0.966)
  Pallas kernels: 22.4 us -> 21.7 us
    pallas_call x1, Pallas kernels: 22.4 us -> 21.7 us  [shards(): pl.pallas_call(functools.partial(kernel, dims), out_shape=pltpu.VMEM((1,...]
where the time goes in v5:
time: 23 us; the launch traced here: 22.9 us
  Pallas kernels  21.7 us (94%)
  between operations  0.66 us (3%)
  local copies, waits for them, and re-layouts  0.51 us (2%)
    pallas_call x1, Pallas kernels, shards(): pl.pallas_call(functools.partial(kernel, dims), out_shape=pltpu.VMEM((1,...  21.7 us
    unnamed x1, local copies, waits for them, and re-layouts  0.51 us

profile of v5, /device:TPU:0, one launch (start us, length us, event | category | flops | bytes accessed | tf_op | source)
XLA Modules:
  0.0 22.9 jit_solution(8500136031564501922)
XLA Ops:
  0.7 21.7 %power_doppler.1 = f32[1,1,16]{2,1,0:T(1,128)S(1)} custom-call(s32[1,2,2]{2,1,0:T(2,128)} %index_hbm.1, s32[1,2,2]{2,1,0:T(2,128)} %live_hbm.1, s32[1,1]{1,0:T(1,128)} %bitcast.3.rank_hbm, bf16[16,128,256]{2,1,0:T(8,128)(2,1)} %bitcast.4, bf16[2,2,128,128]{3,2,1,0:T(8,128)(2,1)} %bitcast.5, f32[32,512]{1,0:T(8,128)} %constant.2.clone.start_hbm), custom_call_target="tpu_custom_call" | custom-call | tf_op jit(solution)/shard_map/power_doppler/pallas_call | solution.py:327
  22.4 0.5 %copy.8 = f32[1,1,16]{2,1,0:T(1,128)} copy(f32[1,1,16]{2,1,0:T(1,128)S(1)} %power_doppler.1) | data formatting | bytes 128

commit v6 on v5

--- a/solution.py
+++ b/solution.py
@@ -146,8 +146,8 @@
 
     def nth_chan(r):
         if n_chan <= 4:
-            c, bit = chan, 1
-            flip = n_chan - 1 - r
+            c, bit, flip = chan, 1, n_chan - 1 - r
+            flip = flip ^ 1 if flip > 1 else flip
             while bit <= flip:
                 if flip & bit:
                     c = c + bit - 2 * bit * lax.rem(chan // bit, 2)
@@ -246,7 +246,7 @@
         else:
             total = lax.fori_loop(1, n, lambda d, t: t + mslots[d], mslots[0])
         unit(full, mine)[...] = total
-        each(n - 1, lambda r: send(unit(full, mine), unit(full, mine), 2, partner(n - 1 - r)).start())
+        each(n - 1, lambda r: send(unit(full, mine), unit(full, mine), 2, partner(r + 1)).start())
         got = mslots.at[pl.ds(0, units - 1)]
         send(got, got, 2, me).wait_recv()
 

time: 23 us -> 22.3 us (0.970)
  Pallas kernels: 21.7 us -> 21 us
    pallas_call x1, Pallas kernels: 21.7 us -> 21 us  [shards(): pl.pallas_call(functools.partial(kernel, dims), out_shape=pltpu.VMEM((1,...]
where the time goes in v6:
time: 22.3 us; the launch traced here: 22.2 us
  Pallas kernels  21 us (94%)
  between operations  0.66 us (3%)
  local copies, waits for them, and re-layouts  0.51 us (2%)
    pallas_call x1, Pallas kernels, shards(): pl.pallas_call(functools.partial(kernel, dims), out_shape=pltpu.VMEM((1,...  21 us
    unnamed x1, local copies, waits for them, and re-layouts  0.51 us

profile of v6, /device:TPU:0, one launch (start us, length us, event | category | flops | bytes accessed | tf_op | source)
XLA Modules:
  0.0 22.2 jit_solution(15837458821852708519)
XLA Ops:
  0.7 21.0 %power_doppler.1 = f32[1,1,16]{2,1,0:T(1,128)S(1)} custom-call(s32[1,2,2]{2,1,0:T(2,128)} %index_hbm.1, s32[1,2,2]{2,1,0:T(2,128)} %live_hbm.1, s32[1,1]{1,0:T(1,128)} %bitcast.3.rank_hbm, bf16[16,128,256]{2,1,0:T(8,128)(2,1)} %bitcast.4, bf16[2,2,128,128]{3,2,1,0:T(8,128)(2,1)} %bitcast.5, f32[32,512]{1,0:T(8,128)} %constant.2.clone.start_hbm), custom_call_target="tpu_custom_call" | custom-call | tf_op jit(solution)/shard_map/power_doppler/pallas_call | solution.py:327
  21.7 0.5 %copy.8 = f32[1,1,16]{2,1,0:T(1,128)} copy(f32[1,1,16]{2,1,0:T(1,128)S(1)} %power_doppler.1) | data formatting | bytes 128

commit v7 on v6

--- a/solution.py
+++ b/solution.py
@@ -212,27 +212,27 @@
     p_high = proj.astype(BF16).astype(F32)
     lane = lax.broadcasted_iota(jnp.int32, proj.shape, 1)
     proj = jnp.where(lane < 2 * vox, p_high, proj - p_high).astype(BF16)
-    sub_part = mm(proj, jnp.concatenate([s_high, s_low] * 2, axis=0), NN)
-    for j in range(n_lane):
-        mpart[j] = sub_part[:, j * LANES : (j + 1) * LANES]
+    stacked = jnp.concatenate([s_high, s_low] * 2, axis=0)
 
     base = (n_chan // 2 - 1) * n_sub * n_frame
     units = n_lane * (RMAX // UNIT)
     reducer = (me >= base) & (me < base + units)
 
     def unit(ref, u):
+        if isinstance(u, int):
+            return ref.at[u // (RMAX // UNIT), pl.ds(u % (RMAX // UNIT) * UNIT, UNIT), :]
         return ref.at[u // (RMAX // UNIT), pl.ds(pl.multiple_of(lax.rem(u, RMAX // UNIT) * UNIT, UNIT), UNIT), :]
 
-    far = jnp.where(me < n // 2, units // 2, 0)
-
-    def to_reducer(r):
-        u = lax.rem(far + r, units)
-
+    def to_reducer(u):
         @pl.when(base + u != me)
         def _():
             send(unit(mpart, u), mslots.at[me], 1, base + u).start()
 
-    each(units, to_reducer)
+    per_lane = RMAX // UNIT
+    for j in range(n_lane):
+        mpart[j] = mm(proj, stacked[:, j * LANES : (j + 1) * LANES], NN)
+        for u in range(j * per_lane, (j + 1) * per_lane):
+            to_reducer(u)
 
     @pl.when(reducer)
     def _():

time: 22.3 us -> 22.3 us (level)
  no operation moved by 1% of the time
where the time goes in v7:
time: 22.3 us; the launch traced here: 22.2 us
  Pallas kernels  21 us (94%)
  between operations  0.66 us (3%)
  local copies, waits for them, and re-layouts  0.51 us (2%)
    pallas_call x1, Pallas kernels, shards(): pl.pallas_call(functools.partial(kernel, dims), out_shape=pltpu.VMEM((1,...  21 us
    unnamed x1, local copies, waits for them, and re-layouts  0.51 us

profile of v7, /device:TPU:0, one launch (start us, length us, event | category | flops | bytes accessed | tf_op | source)
XLA Modules:
  0.0 22.2 jit_solution(16623322030212471764)
XLA Ops:
  0.7 21.0 %power_doppler.1 = f32[1,1,16]{2,1,0:T(1,128)S(1)} custom-call(s32[1,2,2]{2,1,0:T(2,128)} %index_hbm.1, s32[1,2,2]{2,1,0:T(2,128)} %live_hbm.1, s32[1,1]{1,0:T(1,128)} %bitcast.3.rank_hbm, bf16[16,128,256]{2,1,0:T(8,128)(2,1)} %bitcast.4, bf16[2,2,128,128]{3,2,1,0:T(8,128)(2,1)} %bitcast.5, f32[32,512]{1,0:T(8,128)} %constant.2.clone.start_hbm), custom_call_target="tpu_custom_call" | custom-call | tf_op jit(solution)/shard_map/power_doppler/pallas_call | solution.py:327
  21.7 0.5 %copy.8 = f32[1,1,16]{2,1,0:T(1,128)} copy(f32[1,1,16]{2,1,0:T(1,128)S(1)} %power_doppler.1) | data formatting | bytes 128
